TPU v7x, 32 devices: a whole 2x2x4 slice. The times are simulated.
32 devices in a mesh: seq: 8 (over z, y), head: 4 (over x, core).
Axes of the slice: x: 2, y: 2, z: 4, core: 2. Of those that a mesh axis runs over, the one named last changes fastest.
Arguments:
- queries: bfloat16 [16384, 4096], P('seq', 'head'), may hold values from -6 to 6
- key_inputs: bfloat16 [16384, 4096], P('seq', 'head'), may hold values from -6 to 6
- values: bfloat16 [16384, 4096], P('seq', 'head'), may hold values from -36 to 36
- out_gain: float32 [4096], replicated, may hold values from 0.25 to 1.75
Outputs:
- normed: bfloat16 [16384, 4096], P(('seq', 'head'))
All inputs are finite; a program needn't handle non-finite values.
Results may differ from a plain program's by a relative error of at most 0.0056.
Values may be sent and summed in bfloat16 or wider, within the bound.
A program may use at most 64 MiB of HBM per device.

v0:
```python
import jax
import jax.numpy as jnp
from jax import lax
from jax.sharding import PartitionSpec as P

HD = 128
BLOCK = 512


def shards(queries, key_inputs, values, out_gain):
    tok_rows = queries.shape[0]
    feature_count = queries.shape[1]
    local_heads = feature_count // HD
    block_count = tok_rows // BLOCK
    query_map = jax.nn.silu(queries.astype(jnp.float32)).astype(jnp.bfloat16)
    key_map = jax.nn.silu(key_inputs.astype(jnp.float32)).astype(jnp.bfloat16)
    query_map = query_map.reshape(block_count, BLOCK, local_heads, HD)
    key_map = key_map.reshape(block_count, BLOCK, local_heads, HD)
    value_blocks = values.reshape(block_count, BLOCK, local_heads, HD)
    block_states = jnp.einsum(
        "bshd,bshe->bhde", key_map, value_blocks, preferred_element_type=jnp.float32
    )
    running = jnp.cumsum(block_states, axis=0)
    earlier = jnp.concatenate([jnp.zeros_like(block_states[:1]), running[:-1]], axis=0)
    shard_state = running[-1]
    flat_state = shard_state.reshape(1, local_heads * HD * HD)
    slices = lax.all_to_all(flat_state, "seq", split_axis=1, concat_axis=0, tiled=True)
    slice_sums = jnp.cumsum(slices, axis=0)
    before = jnp.concatenate([jnp.zeros_like(slice_sums[:1]), slice_sums[:-1]], axis=0)
    returned = lax.all_to_all(before, "seq", split_axis=0, concat_axis=1, tiled=True)
    prefix = returned.reshape(local_heads, HD, HD)
    states = earlier + prefix[None]
    causal = jnp.tril(jnp.ones((BLOCK, BLOCK), dtype=bool))
    scores = jnp.einsum("bthd,bshd->bhts", query_map, key_map, preferred_element_type=jnp.float32)
    weights = jnp.where(causal[None, None], scores, 0.0).astype(jnp.bfloat16)
    inside = jnp.einsum(
        "bhts,bshd->bthd", weights, value_blocks, preferred_element_type=jnp.float32
    )
    carried = jnp.einsum(
        "bthd,bhde->bthe", query_map.astype(jnp.float32), states, precision=lax.Precision.HIGHEST
    )
    attended = (inside + carried).astype(jnp.bfloat16).reshape(tok_rows, feature_count)
    regrouped = lax.all_to_all(attended, "head", split_axis=0, concat_axis=1, tiled=True)
    wide_out = regrouped.astype(jnp.float32)
    mean_square = jnp.mean(wide_out * wide_out, axis=1, keepdims=True)
    return (wide_out * lax.rsqrt(mean_square + 1e-06) * out_gain).astype(jnp.bfloat16)


def solution(mesh):
    return jax.shard_map(
        shards,
        mesh=mesh,
        in_specs=(P("seq", "head"), P("seq", "head"), P("seq", "head"), P()),
        out_specs=P(("seq", "head"), None),
        check_vma=False,
    )
```

profile of v0, /device:TPU:0, one launch (start us, length us, event | category | flops | bytes accessed | tf_op | source)
XLA Modules:
  0.0 147.9 jit_solution(6072632780366691414)
XLA Ops:
  0.0 3.8 %fusion.14 = bf16[256,8,8,128]{3,1,2,0:T(8,128)(2,1)S(1)} fusion(bf16[2048,1024]{1,0:T(8,128)(2,1)} %param.5), kind=kLoop, calls=%fused_computation.21 | loop fusion | flops 12582912 | bytes 8388608
  3.8 3.1 %copy.24 = bf16[256,8,8,128]{3,2,1,0:T(8,128)(2,1)} copy(bf16[256,8,8,128]{3,1,2,0:T(8,128)(2,1)S(1)} %fusion.14) | data formatting | bytes 8388608
  6.9 7.5 %copy.13 = bf16[4,512,8,128]{1,3,2,0:T(8,128)(2,1)} copy(bf16[4,512,8,128]{3,2,1,0:T(8,128)(2,1)} %bitcast.35) | data formatting | bytes 8388608 | tf_op jit(solution)/shard_map/reshape | solution.py:18
  14.4 0.0 copy-start.1
  14.4 3.5 %copy.25 = bf16[256,8,8,128]{3,2,1,0:T(8,128)(2,1)S(1)} copy(bf16[256,8,8,128]{3,1,2,0:T(8,128)(2,1)} %bitcast.39) | data formatting | bytes 8388608
  17.9 0.0 copy-start.2
  17.9 0.0 copy-done.1
  17.9 1.3 fusion.21
  19.2 0.6 copy-done.2
  19.9 1.3 fusion.30
  21.2 0.0 copy-start.3
  21.2 0.9 slice.13
  22.1 7.3 %all-to-all-start = ((f32[1,8,16384]{2,0,1:T(1,128)}), f32[1,8,16384]{2,0,1:T(1,128)S(1)}, u32[]{:S(2)}, u32[]{:S(2)}) async-start(f32[1,8,16384]{2,0,1:T(1,128)} %bitcast.1), calls=%async_computation | async-start | bytes 1048576 | tf_op jit(solution)/shard_map/all_to_all | solution.py:27
  29.3 3.8 %fusion.15 = bf16[256,8,8,128]{3,1,2,0:T(8,128)(2,1)S(1)} fusion(bf16[2048,1024]{1,0:T(8,128)(2,1)} %param.4), kind=kLoop, calls=%fused_computation.22 | loop fusion | flops 12582912 | bytes 8388608
  33.2 0.0 copy-done.3
  33.2 3.1 %copy.23 = bf16[256,8,8,128]{3,2,1,0:T(8,128)(2,1)} copy(bf16[256,8,8,128]{3,1,2,0:T(8,128)(2,1)S(1)} %fusion.15) | data formatting | bytes 8388608
  36.3 0.1 iota_compare_fusion
  36.4 7.5 %all-to-all-done = f32[1,8,16384]{2,0,1:T(1,128)S(1)} async-done(((f32[1,8,16384]{2,0,1:T(1,128)}), f32[1,8,16384]{2,0,1:T(1,128)S(1)}, u32[]{:S(2)}, u32[]{:S(2)}) %all-to-all-start) | async-done | bytes 524320 | tf_op jit(solution)/shard_map/all_to_all | solution.py:27
  43.8 0.3 copy.38
  44.1 0.5 reduce_window_sum.23
  44.6 0.1 pad_bitcast_fusion
  44.7 1.3 copy.16
  46.0 3.7 %all-to-all-start.1 = ((f32[8,1,16384]{2,1,0:T(1,128)}), f32[8,1,16384]{2,1,0:T(1,128)S(1)}, u32[]{:S(2)}, u32[]{:S(2)}) async-start(f32[8,1,16384]{2,1,0:T(1,128)} %copy.16), calls=%async_computation.1 | async-start | bytes 1048576 | tf_op jit(solution)/shard_map/all_to_all | solution.py:30
  49.7 0.0 slice-start
  49.7 15.3 %fusion = f32[4,8,512,128]{2,3,1,0:T(8,128)} fusion(pred[512,512]{1,0:T(8,128)(4,1)S(1)} %iota_compare_fusion, bf16[4,512,8,128]{1,3,2,0:T(8,128)(2,1)} %copy.13, bf16[4,512,8,128]{3,2,1,0:T(8,128)(2,1)} %bitcast.36, bf16[4,512,8,128]{3,2,1,0:T(8,128)(2,1)} %bitcast.34), kind=kOutput, calls=%fused_computation.1 | convolution fusion | flops 4311744512 | bytes 21233664 | tf_op jit(solution)/shard_map/bhts,bshd->bthd/dot_general | solution.py:36
  65.0 0.0 all-to-all-done.1
  65.0 0.0 slice-done
  65.0 8.7 %fusion.13 = bf16[4,512,8,128]{1,3,2,0:T(8,128)(2,1)S(1)} fusion(f32[4,8,512,128]{2,3,1,0:T(8,128)} %fusion, bf16[4,512,8,128]{3,2,1,0:T(8,128)(2,1)} %bitcast.37, f32[3,8,128,128]{3,2,1,0:T(8,128)S(1)} %slice-done, f32[8,128,128]{2,1,0:T(8,128)S(1)} %bitcast.40), kind=kOutput, calls=%fused_computation.18 | convolution fusion | flops 3225944064 | bytes 18874368 | tf_op jit(solution)/shard_map/bthd,bhde->bthe/dot_general | solution.py:39
  73.7 50.7 %all_to_all.42 = bf16[4,512,1024]{1,2,0:T(8,128)(2,1)S(1)} all-to-all(bf16[4,512,1024]{1,2,0:T(8,128)(2,1)S(1)} %bitcast.38), channel_id=1, replica_groups=mesh['seq'=8,'head'=4] {'head'}, dimensions={0} | all-to-all | bytes 8388608 | tf_op jit(solution)/shard_map/all_to_all | solution.py:43
  124.4 0.0 copy-start
  124.4 4.6 %convert_element_type.47 = f32[4,512,1024]{1,2,0:T(8,128)} convert(bf16[4,512,1024]{1,2,0:T(8,128)(2,1)S(1)} %all_to_all.42) | non-fusion elementwise | flops 2097152 | bytes 12582912 | tf_op jit(solution)/shard_map/convert_element_type | solution.py:44
  129.0 0.0 copy-done
  129.0 9.0 %copy.21 = f32[512,4096]{1,0:T(8,128)} copy(f32[512,4096]{0,1:T(8,128)} %bitcast.32) | data formatting | bytes 16777216 | tf_op jit(solution)/shard_map/convert_element_type | solution.py:44
  138.0 0.0 copy-start.4
  138.0 3.1 %multiply_reduce_fusion = f32[512]{0:T(512)S(1)} fusion(bf16[4,512,1024]{1,2,0:T(8,128)(2,1)} %copy-done), kind=kLoop, calls=%fused_computation.20 | loop fusion | flops 6290944 | bytes 4196352 | tf_op jit(solution)/shard_map/reduce_sum | solution.py:45
  141.2 0.0 copy-done.4
  141.2 6.7 %multiply_convert_fusion = bf16[512,4096]{1,0:T(8,128)(2,1)} fusion(f32[512,4096]{1,0:T(8,128)} %copy.21, f32[4096]{0:T(1024)S(1)} %copy-done.4, f32[512]{0:T(512)S(1)} %add_rsqrt_fusion), kind=kLoop, calls=%fused_computation.19 | loop fusion | flops 6291456 | bytes 12601344 | tf_op jit(solution)/shard_map/convert_element_type | solution.py:46
  (1 shorter events, 0.0 us)
Async XLA Ops:
  14.4 3.5 %copy-start.1 = (bf16[4,512,8,128]{1,3,2,0:T(8,128)(2,1)S(1)}, bf16[4,512,8,128]{1,3,2,0:T(8,128)(2,1)}, u32[]{:S(2)}) copy-start(bf16[4,512,8,128]{1,3,2,0:T(8,128)(2,1)} %copy.13) | copy-start | bytes 12582916
  17.9 1.9 %copy-start.2 = (bf16[256,8,8,128]{3,2,1,0:T(8,128)(2,1)}, bf16[256,8,8,128]{3,2,1,0:T(8,128)(2,1)S(1)}, u32[]{:S(2)}) copy-start(bf16[256,8,8,128]{3,2,1,0:T(8,128)(2,1)S(1)} %copy.25) | copy-start | bytes 12582916
  21.2 12.0 %copy-start.3 = (f32[4,8,128,128]{3,2,1,0:T(8,128)}, f32[4,8,128,128]{3,2,1,0:T(8,128)S(1)}, u32[]{:S(2)}) copy-start(f32[4,8,128,128]{3,2,1,0:T(8,128)S(1)} %fusion.30) | copy-start | bytes 6291460
  22.1 21.8 %all-to-all-start = ((f32[1,8,16384]{2,0,1:T(1,128)}), f32[1,8,16384]{2,0,1:T(1,128)S(1)}, u32[]{:S(2)}, u32[]{:S(2)}) async-start(f32[1,8,16384]{2,0,1:T(1,128)} %bitcast.1), calls=%async_computation | async-start | bytes 1048576 | tf_op jit(solution)/shard_map/all_to_all | solution.py:27
  46.0 19.0 %all-to-all-start.1 = ((f32[8,1,16384]{2,1,0:T(1,128)}), f32[8,1,16384]{2,1,0:T(1,128)S(1)}, u32[]{:S(2)}, u32[]{:S(2)}) async-start(f32[8,1,16384]{2,1,0:T(1,128)} %copy.16), calls=%async_computation.1 | async-start | bytes 1048576 | tf_op jit(solution)/shard_map/all_to_all | solution.py:30
  49.7 15.3 %slice-start = ((f32[4,8,128,128]{3,2,1,0:T(8,128)}), f32[3,8,128,128]{3,2,1,0:T(8,128)S(1)}, s32[]{:S(2)}) async-start(f32[4,8,128,128]{3,2,1,0:T(8,128)} %copy-done.3), calls=%async_computation.3 | async-start | bytes 3145728 | tf_op jit(solution)/shard_map/slice | solution.py:24
  124.4 4.6 %copy-start = (bf16[4,512,1024]{1,2,0:T(8,128)(2,1)}, bf16[4,512,1024]{1,2,0:T(8,128)(2,1)S(1)}, u32[]{:S(2)}) copy-start(bf16[4,512,1024]{1,2,0:T(8,128)(2,1)S(1)} %all_to_all.42) | copy-start | bytes 12582916
  138.0 3.2 %copy-start.4 = (f32[4096]{0:T(1024)S(1)}, f32[4096]{0:T(1024)}, u32[]{:S(2)}) copy-start(f32[4096]{0:T(1024)} %param.7) | copy-start | bytes 49156
where the time goes:
time: 149 us; the launch traced here: 148 us
  blocking collectives  50.7 us (34%)
  local copies, waits for them, and re-layouts  29.4 us (20%)
  matrix products  25.3 us (17%)
  other arithmetic  23.9 us (16%)
  starting transfers between devices  11 us (7%)
  waiting for transfers between devices  7.48 us (5%)
    all_to_all x1, blocking collectives, shards(): lax.all_to_all(attended, 'head', split_axis=0, concat_axis=1, tiled=True)  50.7 us
    dot_general x1, matrix products, shards(): jnp.einsum('bhts,bshd->bthd', weights, value_blocks, preferred_element_ty...  15.3 us
    unnamed x14, local copies, waits for them, and re-layouts  10.6 us
    convert_element_type x1, local copies, waits for them, and re-layouts, shards(): wide_out = regrouped.astype(jnp.float32)  8.97 us
    dot_general x1, matrix products, shards(): jnp.einsum('bthd,bhde->bthe', query_map.astype(jnp.float32), states, prec...  8.69 us
    unnamed x2, other arithmetic  7.6 us
    reshape x1, local copies, waits for them, and re-layouts, shards(): key_map = key_map.reshape(block_count, BLOCK, local_heads, HD)  7.53 us
    all_to_all x1, waiting for transfers between devices, shards(): lax.all_to_all(flat_state, 'seq', split_axis=1, concat_axis=0, tiled=True)  7.48 us
  transfers between devices with their start and end apart: 2, of which 1 were waited for; matrix products, arithmetic and copies ran while one was open for 15% of the time, Pallas kernels for 0%

commit v1 on v0

v1 whole, which is shorter than its diff:
```python
import functools

import jax
import jax.numpy as jnp
from jax import lax
from jax.experimental import pallas as pl
from jax.experimental.pallas import tpu as pltpu
from jax.sharding import PartitionSpec as P

HD = 128
BLOCK = 512
SUB = 256
EPS = 1e-06
FIRST = 2
STEP = 2
NORM_ROWS = 128
MESH = pl.DeviceIdType.MESH


def silu(u):
    wide = u.astype(jnp.float32)
    return (wide * (0.5 + 0.5 * jnp.tanh(0.5 * wide))).astype(jnp.bfloat16)


def attend_kernel(
    seq_n, head_n, q_hbm, k_hbm, v_hbm, out,
    qb, kb, vb, att, before, own, near, far, onward, prefix,
    load_sem, near_send, near_recv, far_send, far_recv, out_send, out_recv, keep_sem,
):
    heads, rows = qb.shape[0], qb.shape[1]
    blocks = rows // BLOCK
    chunk = rows // head_n
    pairs = seq_n // 2
    chips = head_n // 2
    s, me = lax.axis_index("seq"), lax.axis_index("head")
    pair, odd = s // 2, s % 2
    partner = s + 1 - 2 * odd

    def peer(k):
        return ((me // 2 + chips - 1 - k // 2) % chips) * 2 + (me % 2 + 1 - k % 2) % 2

    barrier = pltpu.get_barrier_semaphore()

    def greet(device):
        pl.semaphore_signal(barrier, inc=1, device_id=device, device_id_type=MESH)

    greet({"seq": partner})
    for k in range(head_n - 1):
        greet({"head": peer(k)})

    @pl.when(pair > 0)
    def _():
        greet({"seq": s - 2})

    @pl.when(pair < pairs - 1)
    def _():
        greet({"seq": s + 2})

    def load(which, h):
        src = (q_hbm, k_hbm, v_hbm)[which]
        dst = (qb, kb, vb)[which]
        cols = pl.ds(pl.multiple_of(h * HD, HD), HD)
        return pltpu.make_async_copy(src.at[:, cols], dst.at[h], load_sem.at[which, h])

    for which in (1, 2, 0):
        for h in range(heads):
            if which == 2:
                continue
            load(which, h).start()
            if which == 1:
                load(2, h).start()

    pl.semaphore_wait(
        barrier, head_n + (pair > 0).astype(jnp.int32) + (pair < pairs - 1).astype(jnp.int32)
    )

    def near_copy(h):
        return pltpu.make_async_remote_copy(
            src_ref=own.at[h], dst_ref=near.at[h], send_sem=near_send.at[h],
            recv_sem=near_recv.at[h], device_id={"seq": partner}, device_id_type=MESH,
        )

    def far_copy(h):
        return pltpu.make_async_remote_copy(
            src_ref=onward.at[h], dst_ref=far.at[h], send_sem=far_send.at[h],
            recv_sem=far_recv.at[h], device_id={"seq": s + 2}, device_id_type=MESH,
        )

    def out_copy(h, d):
        first = pl.multiple_of(d * chunk, chunk)
        return pltpu.make_async_remote_copy(
            src_ref=att.at[h, pl.ds(first, chunk)], dst_ref=out.at[me * heads + h],
            send_sem=out_send.at[d, h], recv_sem=out_recv.at[me, h],
            device_id={"head": d}, device_id_type=MESH,
        )

    def in_copy(h, d):
        return pltpu.make_async_remote_copy(
            src_ref=att.at[h, pl.ds(0, chunk)], dst_ref=out.at[d * heads + h],
            send_sem=out_send.at[d, h], recv_sem=out_recv.at[d, h],
            device_id={"head": d}, device_id_type=MESH,
        )

    def keep_copy(h):
        first = pl.multiple_of(me * chunk, chunk)
        return pltpu.make_async_copy(
            att.at[h, pl.ds(first, chunk)], out.at[me * heads + h], keep_sem.at[h]
        )

    def state(h):
        load(1, h).wait()
        load(2, h).wait()
        run = jnp.zeros((HD, HD), jnp.float32)
        for b in range(blocks):
            here = pl.ds(b * BLOCK, BLOCK)
            keys = silu(kb[h, here])
            kb[h, here] = keys
            before[h, b] = run
            run = run + lax.dot_general(
                keys, vb[h, here], (((0,), (0,)), ((), ())), preferred_element_type=jnp.float32
            )
        own[h] = run
        near_copy(h).start()

    def chain(h):
        near_copy(h).wait_recv()
        other = near[h]

        @pl.when(pair > 0)
        def _():
            far_copy(h).wait_recv()

        @pl.when(pair == 0)
        def _():
            far[h] = jnp.zeros((HD, HD), jnp.float32)

        earlier = far[h]

        @pl.when(pair < pairs - 1)
        def _():
            onward[h] = earlier + (own[h] + other)
            far_copy(h).start()

        prefix[h] = earlier + odd.astype(jnp.float32) * other

    def attend(h, row, offset, keys_seen, count, split):
        queries = silu(qb[h, pl.ds(row, count)])
        start = row - offset
        seen = pl.ds(start, keys_seen)
        scores = lax.dot_general(
            queries, kb[h, seen], (((1,), (1,)), ((), ())), preferred_element_type=jnp.float32
        )
        t_pos = lax.broadcasted_iota(jnp.int32, scores.shape, 0) + offset
        s_pos = lax.broadcasted_iota(jnp.int32, scores.shape, 1)
        weights = jnp.where(s_pos <= t_pos, scores, 0.0).astype(jnp.bfloat16)
        total = jnp.dot(weights, vb[h, seen], preferred_element_type=jnp.float32)
        twice = jnp.concatenate([queries, queries], axis=1)
        total = total + jnp.dot(twice, split, preferred_element_type=jnp.float32)
        att[h, pl.ds(row, count)] = total.astype(jnp.bfloat16)

    def split_state(h, b):
        whole = prefix[h] + before[h, b]
        high = whole.astype(jnp.bfloat16)
        low = (whole - high.astype(jnp.float32)).astype(jnp.bfloat16)
        return jnp.concatenate([high, low], axis=0)

    def finish(h):
        load(0, h).wait()

        def serve(k, carry):
            d = peer(k)
            if chunk % BLOCK == 0:
                per = chunk // BLOCK
                for j in range(per):
                    b = d * per + j
                    first = pl.multiple_of(b * BLOCK, BLOCK)
                    split = split_state(h, b)
                    for t in range(BLOCK // SUB):
                        attend(h, first + t * SUB, t * SUB, (t + 1) * SUB, SUB, split)
            else:
                per = BLOCK // chunk
                first = pl.multiple_of(d * chunk, chunk)
                attend(h, first, (d % per) * chunk, BLOCK, chunk, split_state(h, d // per))

            @pl.when(k < head_n - 1)
            def _():
                out_copy(h, d).start()

            @pl.when(k == head_n - 1)
            def _():
                keep_copy(h).start()

            return carry

        lax.fori_loop(0, head_n, serve, 0)

    finish_from = FIRST + STEP * (pairs - 1)

    def slot(i, carry):
        @pl.when(i < heads)
        def _():
            state(i)

        linked = i - FIRST - STEP * pair

        @pl.when((linked >= 0) & (linked < heads))
        def _():
            chain(linked)

        @pl.when((i >= finish_from) & (i < finish_from + heads))
        def _():
            finish(i - finish_from)

        return carry

    lax.fori_loop(0, max(heads, finish_from + heads), slot, 0)

    def drain(h, carry):
        near_copy(h).wait_send()

        @pl.when(pair < pairs - 1)
        def _():
            far_copy(h).wait_send()

        keep_copy(h).wait()
        for k in range(head_n - 1):
            out_copy(h, peer(k)).wait_send()
            in_copy(h, peer(k)).wait_recv()
        return carry

    lax.fori_loop(0, heads, drain, 0)


def norm_kernel(att_ref, gain_ref, out_ref):
    total_heads, rows = att_ref.shape[0], att_ref.shape[1]
    squares = jnp.zeros((rows, HD), jnp.float32)
    for h in range(total_heads):
        wide = att_ref[h].astype(jnp.float32)
        squares = squares + wide * wide
    mean_square = jnp.sum(squares, axis=1, keepdims=True) * (1.0 / (total_heads * HD))
    scale = lax.rsqrt(mean_square + EPS)
    for h in range(total_heads):
        cols = pl.ds(h * HD, HD)
        wide = att_ref[h].astype(jnp.float32)
        out_ref[:, cols] = (wide * scale * gain_ref[:, cols]).astype(jnp.bfloat16)


def shards(seq_n, head_n, queries, key_inputs, values, out_gain):
    rows, features = queries.shape
    heads = features // HD
    chunk = rows // head_n
    total_heads = heads * head_n
    half = pltpu.VMEM((heads, rows, HD), jnp.bfloat16)
    square = pltpu.VMEM((heads, HD, HD), jnp.float32)
    dma = pltpu.SemaphoreType.DMA
    attended = pl.pallas_call(
        functools.partial(attend_kernel, seq_n, head_n),
        out_shape=jax.ShapeDtypeStruct((total_heads, chunk, HD), jnp.bfloat16),
        in_specs=[pl.BlockSpec(memory_space=pl.ANY)] * 3,
        out_specs=pl.BlockSpec(memory_space=pl.ANY),
        scratch_shapes=[
            half, half, half, half,
            pltpu.VMEM((heads, rows // BLOCK, HD, HD), jnp.float32),
            square, square, square, square, square,
            dma((3, heads)), dma((heads,)), dma((heads,)), dma((heads,)), dma((heads,)),
            dma((head_n, heads)), dma((head_n, heads)), dma((heads,)),
        ],
        compiler_params=pltpu.CompilerParams(
            collective_id=0, has_side_effects=True, vmem_limit_bytes=52 * 1024 * 1024
        ),
        name="attend",
    )(queries, key_inputs, values)
    step_rows = min(NORM_ROWS, chunk)
    return pl.pallas_call(
        norm_kernel,
        grid=(chunk // step_rows,),
        out_shape=jax.ShapeDtypeStruct((chunk, total_heads * HD), jnp.bfloat16),
        in_specs=[
            pl.BlockSpec((total_heads, step_rows, HD), lambda i: (0, i, 0)),
            pl.BlockSpec((1, total_heads * HD), lambda i: (0, 0)),
        ],
        out_specs=pl.BlockSpec((step_rows, total_heads * HD), lambda i: (i, 0)),
        compiler_params=pltpu.CompilerParams(vmem_limit_bytes=32 * 1024 * 1024),
        name="norm",
    )(attended, out_gain.reshape(1, -1))


def solution(mesh):
    return jax.shard_map(
        functools.partial(shards, mesh.shape["seq"], mesh.shape["head"]),
        mesh=mesh,
        in_specs=(P("seq", "head"), P("seq", "head"), P("seq", "head"), P()),
        out_specs=P(("seq", "head"), None),
        check_vma=False,
    )
```

time: 149 us -> 69.3 us (0.47)
  Pallas kernels: 0 us -> 66.9 us
  blocking collectives: 50.7 us -> 0 us
  local copies, waits for them, and re-layouts: 29.4 us -> 2.18 us
  matrix products: 25.3 us -> 0 us
  other arithmetic: 23.9 us -> 0 us
  starting transfers between devices: 11 us -> 0 us
  waiting for transfers between devices: 7.48 us -> 0 us
    pallas_call x0 -> x2, Pallas kernels: none -> 66.9 us  [the longest x1 63.3 us: shards(): pl.pallas_call(functools.partial(attend_kernel, seq_n, head_n), out_shape...]
    all_to_all x1 -> x0, blocking collectives: 50.7 us -> none  [shards(): lax.all_to_all(attended, 'head', split_axis=0, concat_axis=1, tiled=True)]
    dot_general x3 -> x0, matrix products: 25.3 us -> none  [the longest x1 15.3 us: shards(): jnp.einsum('bhts,bshd->bthd', weights, value_blocks, preferred_element_ty...]
    convert_element_type x2 -> x0, other arithmetic: 11.3 us -> none  [the longest x1 6.74 us: shards(): (wide_out * lax.rsqrt(mean_square + 1e-06) * out_gain).astype(jnp.bfloat16)]
    all_to_all x2 -> x0, starting transfers between devices: 11 us -> none  [the longest x1 7.28 us: shards(): lax.all_to_all(flat_state, 'seq', split_axis=1, concat_axis=0, tiled=True)]
    convert_element_type x1 -> x0, local copies, waits for them, and re-layouts: 8.97 us -> none  [shards(): wide_out = regrouped.astype(jnp.float32)]
    unnamed x14 -> x4, local copies, waits for them, and re-layouts: 10.6 us -> 2.18 us
    unnamed x2 -> x0, other arithmetic: 7.6 us -> none
  transfers between devices with their start and end apart: 2 -> 0, of which waited for: 1 -> 0; matrix products, arithmetic and copies ran while one was open for 15% -> 0% of each run, Pallas kernels for 0% -> 0%
where the time goes in v1:
time: 69.3 us; the launch traced here: 69.2 us
  Pallas kernels  66.9 us (97%)
  local copies, waits for them, and re-layouts  2.18 us (3%)
    pallas_call x1, Pallas kernels, shards(): pl.pallas_call(functools.partial(attend_kernel, seq_n, head_n), out_shape...  63.3 us
    pallas_call x1, Pallas kernels, shards(): pl.pallas_call(norm_kernel, grid=(chunk // step_rows,), out_shape=jax.Sha...  3.61 us
    unnamed x4, local copies, waits for them, and re-layouts  2.18 us

profile of v1, /device:TPU:0, one launch (start us, length us, event | category | flops | bytes accessed | tf_op | source)
XLA Modules:
  0.0 69.2 jit_solution(8048204802998663295)
XLA Ops:
  0.0 0.0 copy-start.1
  0.0 63.3 %attend.1.att_ref = bf16[32,512,128]{2,1,0:T(8,128)(2,1)} custom-call(bf16[2048,1024]{1,0:T(8,128)(2,1)} %q_hbm.1, bf16[2048,1024]{1,0:T(8,128)(2,1)} %k_hbm.1, bf16[2048,1024]{1,0:T(8,128)(2,1)} %v_hbm.1), custom_call_target="tpu_custom_call" | custom-call | tf_op jit(solution)/shard_map/attend/pallas_call | solution.py:256
  63.3 0.0 copy-done.1
  63.4 0.0 copy-start
  63.4 2.2 %copy-done = bf16[32,512,128]{2,1,0:T(8,128)(2,1)S(1)} copy-done((bf16[32,512,128]{2,1,0:T(8,128)(2,1)S(1)}, bf16[32,512,128]{2,1,0:T(8,128)(2,1)}, u32[]{:S(2)}) %copy-start) | copy-done | bytes 4194328
  65.5 3.6 %norm.1 = bf16[512,4096]{1,0:T(8,128)(2,1)} custom-call(bf16[32,512,128]{2,1,0:T(8,128)(2,1)S(1)} %copy-done, f32[1,4096]{1,0:T(1,128)S(1)} %bitcast.1), custom_call_target="tpu_custom_call" | custom-call | tf_op jit(solution)/shard_map/norm/pallas_call | solution.py:274
Async XLA Ops:
  0.0 63.3 %copy-start.1 = (f32[4096]{0:T(1024)S(1)}, f32[4096]{0:T(1024)}, u32[]{:S(2)}) copy-start(f32[4096]{0:T(1024)} %param.7) | copy-start | bytes 49156
  63.4 2.2 %copy-start = (bf16[32,512,128]{2,1,0:T(8,128)(2,1)S(1)}, bf16[32,512,128]{2,1,0:T(8,128)(2,1)}, u32[]{:S(2)}) copy-start(bf16[32,512,128]{2,1,0:T(8,128)(2,1)} %attend.1.att_ref) | copy-start | bytes 12582916

commit v2 on v1

--- a/solution.py
+++ b/solution.py
@@ -11,9 +11,10 @@
 BLOCK = 512
 SUB = 256
 EPS = 1e-06
-FIRST = 2
-STEP = 2
-NORM_ROWS = 128
+FIRST = 1
+STEP = 1
+BANDS = 4
+NORM_ROWS = 64
 MESH = pl.DeviceIdType.MESH
 
 
@@ -74,16 +75,19 @@
         barrier, head_n + (pair > 0).astype(jnp.int32) + (pair < pairs - 1).astype(jnp.int32)
     )
 
-    def near_copy(h):
+    def band(c):
+        return pl.ds(c * (HD // BANDS), HD // BANDS)
+
+    def near_copy(h, c):
         return pltpu.make_async_remote_copy(
-            src_ref=own.at[h], dst_ref=near.at[h], send_sem=near_send.at[h],
-            recv_sem=near_recv.at[h], device_id={"seq": partner}, device_id_type=MESH,
-        )
-
-    def far_copy(h):
+            src_ref=own.at[h, band(c)], dst_ref=near.at[h, band(c)], send_sem=near_send.at[c, h],
+            recv_sem=near_recv.at[c, h], device_id={"seq": partner}, device_id_type=MESH,
+        )
+
+    def far_copy(h, c):
         return pltpu.make_async_remote_copy(
-            src_ref=onward.at[h], dst_ref=far.at[h], send_sem=far_send.at[h],
-            recv_sem=far_recv.at[h], device_id={"seq": s + 2}, device_id_type=MESH,
+            src_ref=onward.at[h, band(c)], dst_ref=far.at[h, band(c)], send_sem=far_send.at[c, h],
+            recv_sem=far_recv.at[c, h], device_id={"seq": s + 2}, device_id_type=MESH,
         )
 
     def out_copy(h, d):
@@ -120,28 +124,30 @@
                 keys, vb[h, here], (((0,), (0,)), ((), ())), preferred_element_type=jnp.float32
             )
         own[h] = run
-        near_copy(h).start()
+        for c in range(BANDS):
+            near_copy(h, c).start()
 
     def chain(h):
-        near_copy(h).wait_recv()
-        other = near[h]
-
-        @pl.when(pair > 0)
-        def _():
-            far_copy(h).wait_recv()
-
-        @pl.when(pair == 0)
-        def _():
-            far[h] = jnp.zeros((HD, HD), jnp.float32)
-
-        earlier = far[h]
-
-        @pl.when(pair < pairs - 1)
-        def _():
-            onward[h] = earlier + (own[h] + other)
-            far_copy(h).start()
-
-        prefix[h] = earlier + odd.astype(jnp.float32) * other
+        for c in range(BANDS):
+            near_copy(h, c).wait_recv()
+            other = near[h, band(c)]
+
+            @pl.when(pair > 0)
+            def _():
+                far_copy(h, c).wait_recv()
+
+            @pl.when(pair == 0)
+            def _():
+                far[h, band(c)] = jnp.zeros_like(other)
+
+            earlier = far[h, band(c)]
+
+            @pl.when(pair < pairs - 1)
+            def _():
+                onward[h, band(c)] = earlier + (own[h, band(c)] + other)
+                far_copy(h, c).start()
+
+            prefix[h, band(c)] = earlier + odd.astype(jnp.float32) * other
 
     def attend(h, row, offset, keys_seen, count, split):
         queries = silu(qb[h, pl.ds(row, count)])
@@ -216,11 +222,13 @@
     lax.fori_loop(0, max(heads, finish_from + heads), slot, 0)
 
     def drain(h, carry):
-        near_copy(h).wait_send()
+        for c in range(BANDS):
+            near_copy(h, c).wait_send()
 
         @pl.when(pair < pairs - 1)
         def _():
-            far_copy(h).wait_send()
+            for c in range(BANDS):
+                far_copy(h, c).wait_send()
 
         keep_copy(h).wait()
         for k in range(head_n - 1):
@@ -231,18 +239,29 @@
     lax.fori_loop(0, heads, drain, 0)
 
 
-def norm_kernel(att_ref, gain_ref, out_ref):
+def norm_kernel(att_ref, gain_ref, out_hbm, staged, sems):
     total_heads, rows = att_ref.shape[0], att_ref.shape[1]
-    squares = jnp.zeros((rows, HD), jnp.float32)
-    for h in range(total_heads):
-        wide = att_ref[h].astype(jnp.float32)
-        squares = squares + wide * wide
-    mean_square = jnp.sum(squares, axis=1, keepdims=True) * (1.0 / (total_heads * HD))
-    scale = lax.rsqrt(mean_square + EPS)
-    for h in range(total_heads):
-        cols = pl.ds(h * HD, HD)
-        wide = att_ref[h].astype(jnp.float32)
-        out_ref[:, cols] = (wide * scale * gain_ref[:, cols]).astype(jnp.bfloat16)
+    step = rows // sems.shape[0]
+
+    def store(i):
+        here = pl.ds(i * step, step)
+        return pltpu.make_async_copy(staged.at[here], out_hbm.at[here], sems.at[i])
+
+    for i in range(rows // step):
+        here = pl.ds(i * step, step)
+        squares = jnp.zeros((step, HD), jnp.float32)
+        for h in range(total_heads):
+            wide = att_ref[h, here].astype(jnp.float32)
+            squares = squares + wide * wide
+        mean_square = jnp.sum(squares, axis=1, keepdims=True) * (1.0 / (total_heads * HD))
+        scale = jnp.broadcast_to(lax.rsqrt(mean_square + EPS), squares.shape)
+        for h in range(total_heads):
+            cols = pl.ds(h * HD, HD)
+            wide = att_ref[h, here].astype(jnp.float32)
+            staged[here, cols] = (wide * scale * gain_ref[:, cols]).astype(jnp.bfloat16)
+        store(i).start()
+    for i in range(rows // step):
+        store(i).wait()
 
 
 def shards(seq_n, head_n, queries, key_inputs, values, out_gain):
@@ -256,30 +275,30 @@
     attended = pl.pallas_call(
         functools.partial(attend_kernel, seq_n, head_n),
         out_shape=jax.ShapeDtypeStruct((total_heads, chunk, HD), jnp.bfloat16),
-        in_specs=[pl.BlockSpec(memory_space=pl.ANY)] * 3,
-        out_specs=pl.BlockSpec(memory_space=pl.ANY),
+        in_specs=[pl.BlockSpec(memory_space=pltpu.HBM)] * 3,
+        out_specs=pl.BlockSpec(memory_space=pltpu.VMEM),
         scratch_shapes=[
             half, half, half, half,
             pltpu.VMEM((heads, rows // BLOCK, HD, HD), jnp.float32),
             square, square, square, square, square,
-            dma((3, heads)), dma((heads,)), dma((heads,)), dma((heads,)), dma((heads,)),
+            dma((3, heads)), dma((BANDS, heads)), dma((BANDS, heads)),
+            dma((BANDS, heads)), dma((BANDS, heads)),
             dma((head_n, heads)), dma((head_n, heads)), dma((heads,)),
         ],
         compiler_params=pltpu.CompilerParams(
-            collective_id=0, has_side_effects=True, vmem_limit_bytes=52 * 1024 * 1024
+            collective_id=0, has_side_effects=True, vmem_limit_bytes=48 * 1024 * 1024
         ),
         name="attend",
     )(queries, key_inputs, values)
     step_rows = min(NORM_ROWS, chunk)
     return pl.pallas_call(
         norm_kernel,
-        grid=(chunk // step_rows,),
         out_shape=jax.ShapeDtypeStruct((chunk, total_heads * HD), jnp.bfloat16),
-        in_specs=[
-            pl.BlockSpec((total_heads, step_rows, HD), lambda i: (0, i, 0)),
-            pl.BlockSpec((1, total_heads * HD), lambda i: (0, 0)),
+        in_specs=[pl.BlockSpec(memory_space=pltpu.VMEM)] * 2,
+        out_specs=pl.BlockSpec(memory_space=pltpu.HBM),
+        scratch_shapes=[
+            pltpu.VMEM((chunk, total_heads * HD), jnp.bfloat16), dma((chunk // step_rows,)),
         ],
-        out_specs=pl.BlockSpec((step_rows, total_heads * HD), lambda i: (i, 0)),
         compiler_params=pltpu.CompilerParams(vmem_limit_bytes=32 * 1024 * 1024),
         name="norm",
     )(attended, out_gain.reshape(1, -1))

time: 69.3 us -> 62.1 us (0.90)
  Pallas kernels: 66.9 us -> 62 us
  local copies, waits for them, and re-layouts: 2.18 us -> 0.01 us
    pallas_call x1, Pallas kernels: 63.3 us -> 59.6 us  [shards(): pl.pallas_call(functools.partial(attend_kernel, seq_n, head_n), out_shape...]
    unnamed x4 -> x2, local copies, waits for them, and re-layouts: 2.18 us -> 0.01 us
    pallas_call x1, Pallas kernels: 3.61 us -> 2.41 us  [shards(): pl.pallas_call(norm_kernel, out_shape=jax.ShapeDtypeStruct((chunk, total_...]
where the time goes in v2:
time: 62.1 us; the launch traced here: 62 us
  Pallas kernels  62 us (100%)
    pallas_call x1, Pallas kernels, shards(): pl.pallas_call(functools.partial(attend_kernel, seq_n, head_n), out_shape...  59.6 us
    pallas_call x1, Pallas kernels, shards(): pl.pallas_call(norm_kernel, out_shape=jax.ShapeDtypeStruct((chunk, total_...  2.41 us

profile of v2, /device:TPU:0, one launch (start us, length us, event | category | flops | bytes accessed | tf_op | source)
XLA Modules:
  0.0 62.0 jit_solution(6725823561927301234)
XLA Ops:
  0.0 0.0 copy-start
  0.0 59.6 %attend.1.att_ref = bf16[32,512,128]{2,1,0:T(8,128)(2,1)S(1)} custom-call(bf16[2048,1024]{1,0:T(8,128)(2,1)} %q_hbm.1, bf16[2048,1024]{1,0:T(8,128)(2,1)} %k_hbm.1, bf16[2048,1024]{1,0:T(8,128)(2,1)} %v_hbm.1), custom_call_target="tpu_custom_call" | custom-call | tf_op jit(solution)/shard_map/attend/pallas_call | solution.py:275
  59.6 0.0 copy-done
  59.6 2.4 %norm.1 = bf16[512,4096]{1,0:T(8,128)(2,1)} custom-call(bf16[32,512,128]{2,1,0:T(8,128)(2,1)S(1)} %attend.1.att_ref, f32[1,4096]{1,0:T(1,128)S(1)} %bitcast.1), custom_call_target="tpu_custom_call" | custom-call | tf_op jit(solution)/shard_map/norm/pallas_call | solution.py:294
Async XLA Ops:
  0.0 59.6 %copy-start = (f32[4096]{0:T(1024)S(1)}, f32[4096]{0:T(1024)}, u32[]{:S(2)}) copy-start(f32[4096]{0:T(1024)} %param.7) | copy-start | bytes 49156
